TPU v7x, 32 devices: a whole 2x2x4 slice. The times are simulated.
32 devices in a mesh: section: 4 (over x, core), lat: 4 (over z), lon: 2 (over y).
Axes of the slice: x: 2, y: 2, z: 4, core: 2. Of those that a mesh axis runs over, the one named last changes fastest.
Arguments:
- states: bfloat16 [4, 1, 96, 24, 192], P('section', None, 'lat', 'lon'), may hold values from -60 to 60
- loss_grads: bfloat16 [4, 1, 96, 24, 192], P('section', None, 'lat', 'lon'), may hold values from -6 to 6
- land_sea: int32 [96, 24], P('lat', 'lon'), may hold values 0 or 1
- land_embed: float32 [192], replicated, may hold values from -4 to 4
- gain_attn: float32 [192], replicated, may hold values from 0.5 to 1.5
- gain_mlp: float32 [192], replicated, may hold values from 0.5 to 1.5
- w_qkv: bfloat16 [192, 576], replicated, may hold values from -0.4375 to 0.4375
- w_out: bfloat16 [192, 192], replicated, may hold values from -0.4375 to 0.4375
- w_up: bfloat16 [192, 768], replicated, may hold values from -0.4375 to 0.4375
- w_down: bfloat16 [768, 192], replicated, may hold values from -0.21875 to 0.21875
Outputs:
- state_grads: float32 [4, 1, 96, 24, 192], P('section', None, 'lat', 'lon')
- grad_qkv: float32 [192, 576], replicated
- grad_out: float32 [192, 192], replicated
- grad_up: float32 [192, 768], replicated
- grad_down: float32 [768, 192], replicated
- grad_land: float32 [192], replicated
- grad_gain_attn: float32 [192], replicated
- grad_gain_mlp: float32 [192], replicated
All inputs are finite; a program needn't handle non-finite values. No bound on the sum of `land_sea` on one device may be relied on, other than what follows from the above.
Results may differ from a plain program's by a relative error of at most 0.015.
Values may be sent and summed in bfloat16 or wider, within the bound.
A program may use at most 64 MiB of HBM per device.

v0:
```python
import jax
import jax.numpy as jnp
from jax import lax
from jax.sharding import PartitionSpec as P

HEADS = 6
HEAD_DIM = 32
WIN_LAT = 6
WIN_LON = 12


EPS = 1e-05


def shifted(value, axis, steps):
    count = lax.axis_size(axis)
    pairs = [(source, (source + steps) % count) for source in range(count)]
    return lax.ppermute(value, axis, pairs)


def shifted_2(block, axis, distance):
    devices = range(lax.axis_size(axis))
    route = [(i - distance, i) for i in devices if i - distance in devices]
    return lax.ppermute(block, axis, route)


def normalize(field, gain):
    centre = jnp.mean(field, axis=-1, keepdims=True)
    offset = field - centre
    spread = jnp.mean(offset * offset, axis=-1, keepdims=True)
    return offset * lax.rsqrt(spread + EPS) * gain


def exact_gelu(values):
    return jax.nn.gelu(values, approximate=False)


def to_windows(field):
    depth, height, breadth, width = field.shape
    grid = field.reshape(depth, height // WIN_LAT, WIN_LAT, breadth // WIN_LON, WIN_LON, width)
    grid = grid.transpose(1, 3, 0, 2, 4, 5)
    return grid.reshape(height // WIN_LAT, breadth // WIN_LON, depth * WIN_LAT * WIN_LON, width)


def from_windows(blocks, depth):
    band_count, cell_count, tokens, width = blocks.shape
    grid = blocks.reshape(band_count, cell_count, depth, WIN_LAT, WIN_LON, width)
    grid = grid.transpose(2, 0, 3, 1, 4, 5)
    return grid.reshape(depth, band_count * WIN_LAT, cell_count * WIN_LON, width)


def allowed_pairs(first_row, total_rows, band_count, depth):
    row_ids = first_row + jnp.arange(band_count * WIN_LAT, dtype=jnp.int32)
    source = (row_ids + WIN_LAT // 2) % total_rows
    labels = (source < WIN_LAT // 2).astype(jnp.int32).reshape(band_count, 1, WIN_LAT, 1)
    labels = jnp.broadcast_to(labels, (band_count, depth, WIN_LAT, WIN_LON))
    labels = labels.reshape(band_count, depth * WIN_LAT * WIN_LON)
    return (labels[:, :, None] == labels[:, None, :]).astype(jnp.float32)


def heads_of(block):
    band_count, cell_count, tokens, width = block.shape
    return block.reshape(band_count, cell_count, tokens, HEADS, width // HEADS)


def merge_heads(block):
    band_count, cell_count, tokens, heads, size = block.shape
    return block.reshape(band_count, cell_count, tokens, heads * size)


def attend(qkv_win, allow):
    width = qkv_win.shape[-1] // 3
    query = heads_of(qkv_win[..., :width])
    keys = heads_of(qkv_win[..., width : 2 * width])
    values = heads_of(qkv_win[..., 2 * width :])
    scores = jnp.einsum(
        "abqhd,abkhd->abhqk", query, keys, preferred_element_type=jnp.float32
    ) * HEAD_DIM ** (-0.5)
    weights = jnp.exp(scores) * allow[:, None, None]
    probs = weights / jnp.sum(weights, axis=-1, keepdims=True)
    mixed = jnp.einsum(
        "abhqk,abkhd->abqhd", probs.astype(jnp.bfloat16), values, preferred_element_type=jnp.float32
    )
    return (probs, merge_heads(mixed).astype(jnp.bfloat16))


def attend_back(qkv_win, probs, d_mixed):
    width = qkv_win.shape[-1] // 3
    query = heads_of(qkv_win[..., :width])
    keys = heads_of(qkv_win[..., width : 2 * width])
    values = heads_of(qkv_win[..., 2 * width :])
    d_heads = heads_of(d_mixed)
    d_probs = jnp.einsum("abqhd,abkhd->abhqk", d_heads, values, preferred_element_type=jnp.float32)
    d_values = jnp.einsum(
        "abhqk,abqhd->abkhd",
        probs.astype(jnp.bfloat16),
        d_heads,
        preferred_element_type=jnp.float32,
    )
    d_scores = (
        probs * (d_probs - jnp.sum(probs * d_probs, axis=-1, keepdims=True)) * HEAD_DIM ** (-0.5)
    )
    d_scores = d_scores.astype(jnp.bfloat16)
    d_query = jnp.einsum("abhqk,abkhd->abqhd", d_scores, keys, preferred_element_type=jnp.float32)
    d_keys = jnp.einsum("abhqk,abqhd->abkhd", d_scores, query, preferred_element_type=jnp.float32)
    joined = jnp.concatenate(
        [merge_heads(d_query), merge_heads(d_keys), merge_heads(d_values)], axis=-1
    )
    return joined.astype(jnp.bfloat16)


def rows_ahead(field):
    half = WIN_LAT // 2
    piece = field[:, :half]
    arrived = shifted(piece, "lat", -1)
    return jnp.concatenate([field[:, half:], arrived], axis=1)


def rows_behind(field):
    half = WIN_LAT // 2
    piece = field[:, -half:]
    arrived = shifted(piece, "lat", 1)
    return jnp.concatenate([arrived, field[:, :-half]], axis=1)


def cols_ahead(field):
    half = WIN_LON // 2
    arrived = shifted(field[:, :, :half], "lon", -1)
    return jnp.concatenate([field[:, :, half:], arrived], axis=2)


def cols_behind(field):
    half = WIN_LON // 2
    arrived = shifted(field[:, :, -half:], "lon", 1)
    return jnp.concatenate([arrived, field[:, :, :-half]], axis=2)


def roll_ahead(field):
    return cols_ahead(rows_ahead(field))


def roll_behind(field):
    return cols_behind(rows_behind(field))


def forward(
    state, land, first_row, total_rows, land_embed, gain_attn, gain_mlp, w_qkv, w_out, w_up
):
    depth, height, breadth, width = state.shape
    embedded = state.astype(jnp.float32) + land * land_embed
    normed, attn_back = jax.vjp(normalize, embedded, gain_attn)
    normed = normed.astype(jnp.bfloat16)
    rolled = roll_ahead(normed).reshape(-1, width)
    qkv = jnp.dot(rolled, w_qkv, preferred_element_type=jnp.float32).astype(jnp.bfloat16)
    qkv_win = to_windows(qkv.reshape(depth, height, breadth, 3 * width))
    allow = allowed_pairs(first_row, total_rows, height // WIN_LAT, depth)
    probs, mixed_win = attend(qkv_win, allow)
    mixed = from_windows(mixed_win, depth).reshape(-1, width)
    projected = jnp.dot(mixed, w_out, preferred_element_type=jnp.float32).astype(jnp.bfloat16)
    hidden_in = embedded + roll_behind(projected.reshape(depth, height, breadth, width)).astype(
        jnp.float32
    )
    normed_mlp, mlp_back = jax.vjp(normalize, hidden_in, gain_mlp)
    normed_mlp = normed_mlp.astype(jnp.bfloat16).reshape(-1, width)
    pre_act = jnp.dot(normed_mlp, w_up, preferred_element_type=jnp.float32)
    activated, gelu_back = jax.vjp(exact_gelu, pre_act)
    activated = activated.astype(jnp.bfloat16)
    return (attn_back, rolled, qkv_win, probs, mixed, mlp_back, normed_mlp, gelu_back, activated)


def backward(saved, cotangent, land, w_qkv, w_out, w_up, w_down, with_weights):
    attn_back, rolled, qkv_win, probs, mixed, mlp_back, normed_mlp, gelu_back, activated = saved
    depth, height, breadth, width = cotangent.shape
    cot_round = cotangent.astype(jnp.bfloat16).reshape(-1, width)
    d_act = jnp.dot(cot_round, w_down.T, preferred_element_type=jnp.float32)
    d_pre = gelu_back(d_act)[0].astype(jnp.bfloat16)
    d_normed_mlp = jnp.dot(d_pre, w_up.T, preferred_element_type=jnp.float32).reshape(
        depth, height, breadth, width
    )
    d_hidden, gain_mlp_part = mlp_back(d_normed_mlp)
    d_hidden = cotangent + d_hidden
    d_projected = roll_ahead(d_hidden.astype(jnp.bfloat16)).reshape(-1, width)
    d_mixed = jnp.dot(d_projected, w_out.T, preferred_element_type=jnp.float32).astype(jnp.bfloat16)
    d_qkv_win = attend_back(
        qkv_win, probs, to_windows(d_mixed.reshape(depth, height, breadth, width))
    )
    d_qkv = from_windows(d_qkv_win, depth).reshape(-1, 3 * width)
    d_rolled = jnp.dot(d_qkv, w_qkv.T, preferred_element_type=jnp.float32).astype(jnp.bfloat16)
    d_normed = roll_behind(d_rolled.reshape(depth, height, breadth, width)).astype(jnp.float32)
    d_embedded, gain_attn_part = attn_back(d_normed)
    d_state = d_hidden + d_embedded
    if not with_weights:
        return (d_state, None)
    part_down = jnp.dot(activated.T, cot_round, preferred_element_type=jnp.float32)
    part_up = jnp.dot(normed_mlp.T, d_pre, preferred_element_type=jnp.float32)
    part_out = jnp.dot(mixed.T, d_projected, preferred_element_type=jnp.float32)
    part_qkv = jnp.dot(rolled.T, d_qkv, preferred_element_type=jnp.float32)
    part_land = jnp.sum(d_state * land, axis=(0, 1, 2))
    return (
        d_state,
        (part_qkv, part_out, part_up, part_down, part_land, gain_attn_part, gain_mlp_part),
    )


def local(
    states, loss_grads, land_sea, land_embed, gain_attn, gain_mlp, w_qkv, w_out, w_up, w_down
):
    depth = states.shape[1]
    band_rows = states.shape[2]
    breadth = states.shape[3]
    total_rows = band_rows * lax.axis_size("lat")
    section_count = lax.axis_size("section")
    land = land_sea.astype(jnp.float32)[None, :, :, None]
    first_row = lax.axis_index("lat") * band_rows
    saved = forward(
        states[0], land, first_row, total_rows, land_embed, gain_attn, gain_mlp, w_qkv, w_out, w_up
    )
    own_loss = loss_grads[0].astype(jnp.float32)
    incoming = jnp.zeros(own_loss.shape, jnp.float32)
    for number in range(section_count - 1):
        d_state, unused = backward(
            saved, own_loss + incoming, land, w_qkv, w_out, w_up, w_down, False
        )
        incoming = shifted_2(d_state.astype(jnp.bfloat16), "section", -1).astype(jnp.float32)
    d_state, parts = backward(saved, own_loss + incoming, land, w_qkv, w_out, w_up, w_down, True)
    d_out = d_state[None]
    totals = lax.psum(
        (parts[0], parts[1], parts[2], parts[3], parts[4], parts[5], parts[6]),
        ("section", "lat", "lon"),
    )
    cell_total = section_count * depth * total_rows * breadth * lax.axis_size("lon")
    factor = float(cell_total) ** (-0.5)
    return (
        d_out,
        totals[0] * factor,
        totals[1] * factor,
        totals[2] * factor,
        totals[3] * factor,
        totals[4] * factor,
        totals[5] * factor,
        totals[6] * factor,
    )


def solution(mesh):
    return jax.shard_map(
        local,
        mesh=mesh,
        in_specs=(
            P("section", None, "lat", "lon", None),
            P("section", None, "lat", "lon", None),
            P("lat", "lon"),
            P(),
            P(),
            P(),
            P(),
            P(),
            P(),
            P(),
        ),
        out_specs=(P("section", None, "lat", "lon", None), P(), P(), P(), P(), P(), P(), P()),
        check_vma=False,
    )
```

profile of v0, /device:TPU:1, one launch (start us, length us, event | category | flops | bytes accessed | tf_op | source)
XLA Modules:
  0.0 343.1 jit_solution(6705967245656341233)
XLA Ops:
  8.1 1.1 fusion.123
  11.1 4.2 %collective-permute-start = (bf16[1,3,12,192]{3,2,1,0:T(8,128)(2,1)S(1)}, bf16[1,3,12,192]{3,2,1,0:T(8,128)(2,1)S(1)}, u32[]{:S(2)}, u32[]{:S(2)}) collective-permute-start(bf16[1,3,12,192]{3,2,1,0:T(8,128)(2,1)S(1)} %slice.185), channel_id=1, source_target_pairs={{0,6},{2,0},{4,2},{6,4},{1,7},{3,1},{5,3},{7,5},{8,14},{10,8},{12,... | collective-permute-start | bytes 41480 | tf_op jit(solution)/shard_map/ppermute | solution.py:18
  16.3 1.3 collective-permute-start.1
  17.7 2.1 collective-permute-done.1
  22.1 1.4 fusion.206
  25.7 4.7 %collective-permute-done.2 = bf16[1,3,12,192]{3,2,1,0:T(8,128)(2,1)S(1)} collective-permute-done((bf16[1,3,12,192]{3,2,1,0:T(8,128)(2,1)S(1)}, bf16[1,3,12,192]{3,2,1,0:T(8,128)(2,1)S(1)}, u32[]{:S(2)}, u32[]{:S(2)}) %collective-permute-start.2) | collective-permute-done | bytes 13856 | tf_op jit(solution)/shard_map/ppermute | solution.py:18
  30.5 1.3 collective-permute-start.3
  32.7 1.3 collective-permute-done.3
  35.6 3.2 fusion.35
  38.8 2.0 fusion.43
  42.0 1.6 collective-permute-start.4
  43.7 1.1 collective-permute-done.4
  44.8 1.3 collective-permute-start.5
  46.1 2.2 collective-permute-done.5
  49.4 1.4 fusion.150
  50.7 2.3 fusion.23
  53.1 2.3 fusion.24
  56.4 1.0 convolution_convert_fusion.17
  58.7 4.6 %collective-permute-done.6 = bf16[1,3,12,192]{3,2,1,0:T(8,128)(2,1)S(1)} collective-permute-done((bf16[1,3,12,192]{3,2,1,0:T(8,128)(2,1)S(1)}, bf16[1,3,12,192]{3,2,1,0:T(8,128)(2,1)S(1)}, u32[]{:S(2)}, u32[]{:S(2)}) %collective-permute-start.6) | collective-permute-done | bytes 13856 | tf_op jit(solution)/shard_map/ppermute | solution.py:18
  63.3 1.3 collective-permute-start.7
  64.6 2.2 collective-permute-done.7
  68.4 11.4 %collective-permute-start.8 = (bf16[1,24,12,192]{3,2,1,0:T(8,128)(2,1)S(1)}, bf16[1,24,12,192]{3,2,1,0:T(8,128)(2,1)S(1)}, u32[]{:S(2)}, u32[]{:S(2)}) collective-permute-start(bf16[1,24,12,192]{3,2,1,0:T(8,128)(2,1)S(1)} %add_convert_fusion.6), channel_id=1, source_target_pairs={{8,0},{16,8},{24,16},{9,1},{17,9},{25,17},{10,2},{18,10},{26,18},{... | collective-permute-start | bytes 331784 | tf_op jit(solution)/shard_map/ppermute | solution.py:24
  79.8 4.4 %collective-permute-done.8 = bf16[1,24,12,192]{3,2,1,0:T(8,128)(2,1)S(1)} collective-permute-done((bf16[1,24,12,192]{3,2,1,0:T(8,128)(2,1)S(1)}, bf16[1,24,12,192]{3,2,1,0:T(8,128)(2,1)S(1)}, u32[]{:S(2)}, u32[]{:S(2)}) %collective-permute-start.8) | collective-permute-done | bytes 110624 | tf_op jit(solution)/shard_map/ppermute | solution.py:24
  85.2 2.0 fusion.37
  88.5 1.8 collective-permute-start.9
  91.3 1.3 collective-permute-start.10
  92.6 2.2 collective-permute-done.10
  95.8 1.4 fusion.147
  97.2 2.4 fusion.26
  99.6 3.0 fusion.27
  105.8 1.0 convolution_convert_fusion.16
  107.9 4.7 %collective-permute-done.11 = bf16[1,3,12,192]{3,2,1,0:T(8,128)(2,1)S(1)} collective-permute-done((bf16[1,3,12,192]{3,2,1,0:T(8,128)(2,1)S(1)}, bf16[1,3,12,192]{3,2,1,0:T(8,128)(2,1)S(1)}, u32[]{:S(2)}, u32[]{:S(2)}) %collective-permute-start.11) | collective-permute-done | bytes 13856 | tf_op jit(solution)/shard_map/ppermute | solution.py:18
  112.7 1.3 collective-permute-start.12
  114.0 3.0 collective-permute-done.12
  118.6 2.9 collective-permute-start.13
  121.5 5.8 %collective-permute-done.13 = bf16[1,24,12,192]{3,2,1,0:T(8,128)(2,1)S(1)} collective-permute-done((bf16[1,24,12,192]{3,2,1,0:T(8,128)(2,1)S(1)}, bf16[1,24,12,192]{3,2,1,0:T(8,128)(2,1)S(1)}, u32[]{:S(2)}, u32[]{:S(2)}) %collective-permute-start.13) | collective-permute-done | bytes 110624 | tf_op jit(solution)/shard_map/ppermute | solution.py:24
  128.2 2.0 fusion.36
  131.5 1.8 collective-permute-start.14
  133.3 1.2 collective-permute-done.14
  134.6 1.3 collective-permute-start.15
  135.9 2.2 collective-permute-done.15
  139.1 1.4 fusion.144
  140.5 2.4 fusion.29
  142.9 3.0 fusion.30
  149.1 1.0 convolution_convert_fusion.15
  151.4 4.4 %collective-permute-done.16 = bf16[1,3,12,192]{3,2,1,0:T(8,128)(2,1)S(1)} collective-permute-done((bf16[1,3,12,192]{3,2,1,0:T(8,128)(2,1)S(1)}, bf16[1,3,12,192]{3,2,1,0:T(8,128)(2,1)S(1)}, u32[]{:S(2)}, u32[]{:S(2)}) %collective-permute-start.16) | collective-permute-done | bytes 13856 | tf_op jit(solution)/shard_map/ppermute | solution.py:18
  155.9 1.3 collective-permute-start.17
  157.2 2.5 collective-permute-done.17
  161.4 1.9 collective-permute-start.18
  163.3 7.1 %collective-permute-done.18 = bf16[1,24,12,192]{3,2,1,0:T(8,128)(2,1)S(1)} collective-permute-done((bf16[1,24,12,192]{3,2,1,0:T(8,128)(2,1)S(1)}, bf16[1,24,12,192]{3,2,1,0:T(8,128)(2,1)S(1)}, u32[]{:S(2)}, u32[]{:S(2)}) %collective-permute-start.18) | collective-permute-done | bytes 110624 | tf_op jit(solution)/shard_map/ppermute | solution.py:24
  172.1 1.9 add_convert_fusion
  176.1 1.8 collective-permute-start.19
  177.9 2.1 fusion.70
  180.1 1.3 collective-permute-start.20
  181.4 1.3 fusion.197
  185.6 1.8 fusion.32
  187.4 1.8 fusion.33
  192.4 1.1 fusion.208
  193.6 2.5 collective-permute-done.21
  196.2 1.3 collective-permute-start.22
  198.4 1.3 collective-permute-done.22
  201.6 39.6 %all-reduce = (f32[192]{0:T(256)S(1)}, f32[192]{0:T(256)S(1)}, f32[192]{0:T(256)S(1)}) all-reduce(f32[192]{0:T(256)S(1)} %get-tuple-element.19, f32[192]{0:T(256)S(1)} %get-tuple-element.18, f32[192]{0:T(256)S(1)} %get-tuple-element.16), channel_id=1, replica_groups=mesh['section'=4,'lat'=4,'lon'=2] {'section','lat','lon'}, use_global_device_ids=true, to_apply=%region_30.31 | all-reduce | flops 576 | bytes 4608 | tf_op jit(solution)/shard_map/psum | solution.py:227
  242.4 89.1 %all-reduce.4.cloned.1.call-done = (f32[192,576]{1,0:T(8,128)}, f32[192,192]{1,0:T(8,128)}, f32[192,768]{1,0:T(8,128)}, f32[768,192]{0,1:T(8,128)}) async-done(((f32[192,576]{1,0:T(8,128)}, f32[192,192]{1,0:T(8,128)}, f32[192,768]{1,0:T(8,128)}, f32[768,192]{0,1:T(8,128)}), (f32[192,576]{1,0:T(8,128)}, f32[192,192]{1,0:T(8,128)}, f32[192,768]{1,0:T(8,128)}, ...) | async-done | bytes 1769488 | tf_op jit(solution)/shard_map/psum | solution.py:227
  331.5 1.9 broadcast_multiply_fusion.2
  (283 shorter events, 52.4 us)
Async XLA Ops:
  7.2 27.9 %copy-start = (bf16[192,768]{1,0:T(8,128)(2,1)S(1)}, bf16[192,768]{1,0:T(8,128)(2,1)}, u32[]{:S(2)}) copy-start(bf16[192,768]{1,0:T(8,128)(2,1)} %param.18) | copy-start | bytes 884740
  7.2 2.1 copy-start.1
  7.2 324.3 %all-reduce.4.cloned.1.call-start = ((), (), s32[]{:S(2)}) async-start(), calls=%async_computation | async-start | bytes 3735552 | tf_op jit(solution)/shard_map/psum | solution.py:227
  9.2 0.7 copy-start.14
  10.2 0.7 copy-start.29
  11.1 5.2 %collective-permute-start = (bf16[1,3,12,192]{3,2,1,0:T(8,128)(2,1)S(1)}, bf16[1,3,12,192]{3,2,1,0:T(8,128)(2,1)S(1)}, u32[]{:S(2)}, u32[]{:S(2)}) collective-permute-start(bf16[1,3,12,192]{3,2,1,0:T(8,128)(2,1)S(1)} %slice.185), channel_id=1, source_target_pairs={{0,6},{2,0},{4,2},{6,4},{1,7},{3,1},{5,3},{7,5},{8,14},{10,8},{12,... | collective-permute-start | bytes 41480 | tf_op jit(solution)/shard_map/ppermute | solution.py:18
  16.3 3.5 %collective-permute-start.1 = (bf16[1,24,6,192]{3,2,1,0:T(8,128)(2,1)S(1)}, bf16[1,24,6,192]{3,2,1,0:T(8,128)(2,1)S(1)}, u32[]{:S(2)}, u32[]{:S(2)}) collective-permute-start(bf16[1,24,6,192]{3,2,1,0:T(8,128)(2,1)S(1)} %get-tuple-element.42), channel_id=1, source_target_pairs={{0,1},{1,0},{2,3},{3,2},{4,5},{5,4},{6,7},{7,6},{8,9},{9,8},{10,11... | collective-permute-start | bytes 165896 | tf_op jit(solution)/shard_map/ppermute | solution.py:18
  19.9 0.9 copy-start.8
  20.8 0.6 copy-start.6
  21.8 29.0 %copy-start.22 = (bf16[4,1,72,192]{2,3,0,1:T(8,128)(2,1)}, bf16[4,1,72,192]{2,3,0,1:T(8,128)(2,1)S(1)}, u32[]{:S(2)}) copy-start(bf16[4,1,72,192]{2,3,0,1:T(8,128)(2,1)S(1)} %copy.64) | copy-start | bytes 331780
  22.0 1.6 copy-start.24
  24.0 0.9 copy-start.3
  24.9 0.7 copy-start.4
  25.6 4.8 %collective-permute-start.2 = (bf16[1,3,12,192]{3,2,1,0:T(8,128)(2,1)S(1)}, bf16[1,3,12,192]{3,2,1,0:T(8,128)(2,1)S(1)}, u32[]{:S(2)}, u32[]{:S(2)}) collective-permute-start(bf16[1,3,12,192]{3,2,1,0:T(8,128)(2,1)S(1)} %slice.191), channel_id=1, source_target_pairs={{0,2},{2,4},{4,6},{6,0},{1,3},{3,5},{5,7},{7,1},{8,10},{10,12},{12... | collective-permute-start | bytes 41480 | tf_op jit(solution)/shard_map/ppermute | solution.py:18
  30.5 1.5 copy-start.2
  30.5 3.5 %collective-permute-start.3 = (bf16[1,24,6,192]{3,2,1,0:T(8,128)(2,1)S(1)}, bf16[1,24,6,192]{3,2,1,0:T(8,128)(2,1)S(1)}, u32[]{:S(2)}, u32[]{:S(2)}) collective-permute-start(bf16[1,24,6,192]{3,2,1,0:T(8,128)(2,1)S(1)} %fusion.160), channel_id=1, source_target_pairs={{0,1},{1,0},{2,3},{3,2},{4,5},{5,4},{6,7},{7,6},{8,9},{9,8},{10,11... | collective-permute-start | bytes 165896 | tf_op jit(solution)/shard_map/ppermute | solution.py:18
  34.9 0.7 copy-start.18
  35.6 3.2 copy-start.30
  35.6 3.2 copy-start.35
  42.0 2.7 collective-permute-start.4
  44.8 3.5 %collective-permute-start.5 = (bf16[1,24,6,192]{3,2,1,0:T(8,128)(2,1)S(1)}, bf16[1,24,6,192]{3,2,1,0:T(8,128)(2,1)S(1)}, u32[]{:S(2)}, u32[]{:S(2)}) collective-permute-start(bf16[1,24,6,192]{3,2,1,0:T(8,128)(2,1)S(1)} %get-tuple-element.40), channel_id=1, source_target_pairs={{0,1},{1,0},{2,3},{3,2},{4,5},{5,4},{6,7},{7,6},{8,9},{9,8},{10,11... | collective-permute-start | bytes 165896 | tf_op jit(solution)/shard_map/ppermute | solution.py:18
  50.7 2.4 copy-start.25
  58.4 4.8 %collective-permute-start.6 = (bf16[1,3,12,192]{3,2,1,0:T(8,128)(2,1)S(1)}, bf16[1,3,12,192]{3,2,1,0:T(8,128)(2,1)S(1)}, u32[]{:S(2)}, u32[]{:S(2)}) collective-permute-start(bf16[1,3,12,192]{3,2,1,0:T(8,128)(2,1)S(1)} %slice.199), channel_id=1, source_target_pairs={{0,2},{2,4},{4,6},{6,0},{1,3},{3,5},{5,7},{7,1},{8,10},{10,12},{12... | collective-permute-start | bytes 41480 | tf_op jit(solution)/shard_map/ppermute | solution.py:18
  63.3 3.5 %collective-permute-start.7 = (bf16[1,24,6,192]{3,2,1,0:T(8,128)(2,1)S(1)}, bf16[1,24,6,192]{3,2,1,0:T(8,128)(2,1)S(1)}, u32[]{:S(2)}, u32[]{:S(2)}) collective-permute-start(bf16[1,24,6,192]{3,2,1,0:T(8,128)(2,1)S(1)} %fusion.158), channel_id=1, source_target_pairs={{0,1},{1,0},{2,3},{3,2},{4,5},{5,4},{6,7},{7,6},{8,9},{9,8},{10,11... | collective-permute-start | bytes 165896 | tf_op jit(solution)/shard_map/ppermute | solution.py:18
  68.4 15.8 %collective-permute-start.8 = (bf16[1,24,12,192]{3,2,1,0:T(8,128)(2,1)S(1)}, bf16[1,24,12,192]{3,2,1,0:T(8,128)(2,1)S(1)}, u32[]{:S(2)}, u32[]{:S(2)}) collective-permute-start(bf16[1,24,12,192]{3,2,1,0:T(8,128)(2,1)S(1)} %add_convert_fusion.6), channel_id=1, source_target_pairs={{8,0},{16,8},{24,16},{9,1},{17,9},{25,17},{10,2},{18,10},{26,18},{... | collective-permute-start | bytes 331784 | tf_op jit(solution)/shard_map/ppermute | solution.py:24
  84.3 1.0 copy-start.36
  88.5 2.7 collective-permute-start.9
  91.3 3.5 %collective-permute-start.10 = (bf16[1,24,6,192]{3,2,1,0:T(8,128)(2,1)S(1)}, bf16[1,24,6,192]{3,2,1,0:T(8,128)(2,1)S(1)}, u32[]{:S(2)}, u32[]{:S(2)}) collective-permute-start(bf16[1,24,6,192]{3,2,1,0:T(8,128)(2,1)S(1)} %get-tuple-element.38), channel_id=1, source_target_pairs={{0,1},{1,0},{2,3},{3,2},{4,5},{5,4},{6,7},{7,6},{8,9},{9,8},{10,11... | collective-permute-start | bytes 165896 | tf_op jit(solution)/shard_map/ppermute | solution.py:18
  97.2 2.4 copy-start.26
  102.8 0.9 copy-start.20
  104.9 0.9 copy-start.31
  104.9 1.0 copy-start.33
  107.8 4.8 %collective-permute-start.11 = (bf16[1,3,12,192]{3,2,1,0:T(8,128)(2,1)S(1)}, bf16[1,3,12,192]{3,2,1,0:T(8,128)(2,1)S(1)}, u32[]{:S(2)}, u32[]{:S(2)}) collective-permute-start(bf16[1,3,12,192]{3,2,1,0:T(8,128)(2,1)S(1)} %slice.207), channel_id=1, source_target_pairs={{0,2},{2,4},{4,6},{6,0},{1,3},{3,5},{5,7},{7,1},{8,10},{10,12},{12... | collective-permute-start | bytes 41480 | tf_op jit(solution)/shard_map/ppermute | solution.py:18
  112.7 4.3 %collective-permute-start.12 = (bf16[1,24,6,192]{3,2,1,0:T(8,128)(2,1)S(1)}, bf16[1,24,6,192]{3,2,1,0:T(8,128)(2,1)S(1)}, u32[]{:S(2)}, u32[]{:S(2)}) collective-permute-start(bf16[1,24,6,192]{3,2,1,0:T(8,128)(2,1)S(1)} %fusion.156), channel_id=1, source_target_pairs={{0,1},{1,0},{2,3},{3,2},{4,5},{5,4},{6,7},{7,6},{8,9},{9,8},{10,11... | collective-permute-start | bytes 165896 | tf_op jit(solution)/shard_map/ppermute | solution.py:18
  118.6 8.6 %collective-permute-start.13 = (bf16[1,24,12,192]{3,2,1,0:T(8,128)(2,1)S(1)}, bf16[1,24,12,192]{3,2,1,0:T(8,128)(2,1)S(1)}, u32[]{:S(2)}, u32[]{:S(2)}) collective-permute-start(bf16[1,24,12,192]{3,2,1,0:T(8,128)(2,1)S(1)} %add_convert_fusion.5), channel_id=1, source_target_pairs={{8,0},{16,8},{24,16},{9,1},{17,9},{25,17},{10,2},{18,10},{26,18},{... | collective-permute-start | bytes 331784 | tf_op jit(solution)/shard_map/ppermute | solution.py:24
  127.3 1.0 copy-start.37
  131.5 3.0 collective-permute-start.14
  134.6 3.5 %collective-permute-start.15 = (bf16[1,24,6,192]{3,2,1,0:T(8,128)(2,1)S(1)}, bf16[1,24,6,192]{3,2,1,0:T(8,128)(2,1)S(1)}, u32[]{:S(2)}, u32[]{:S(2)}) collective-permute-start(bf16[1,24,6,192]{3,2,1,0:T(8,128)(2,1)S(1)} %get-tuple-element.36), channel_id=1, source_target_pairs={{0,1},{1,0},{2,3},{3,2},{4,5},{5,4},{6,7},{7,6},{8,9},{9,8},{10,11... | collective-permute-start | bytes 165896 | tf_op jit(solution)/shard_map/ppermute | solution.py:18
  140.5 2.4 copy-start.27
  146.1 0.9 copy-start.21
  148.2 0.9 copy-start.32
  148.2 1.0 copy-start.34
  151.1 4.7 %collective-permute-start.16 = (bf16[1,3,12,192]{3,2,1,0:T(8,128)(2,1)S(1)}, bf16[1,3,12,192]{3,2,1,0:T(8,128)(2,1)S(1)}, u32[]{:S(2)}, u32[]{:S(2)}) collective-permute-start(bf16[1,3,12,192]{3,2,1,0:T(8,128)(2,1)S(1)} %slice.215), channel_id=1, source_target_pairs={{0,2},{2,4},{4,6},{6,0},{1,3},{3,5},{5,7},{7,1},{8,10},{10,12},{12... | collective-permute-start | bytes 41480 | tf_op jit(solution)/shard_map/ppermute | solution.py:18
  155.9 3.9 %collective-permute-start.17 = (bf16[1,24,6,192]{3,2,1,0:T(8,128)(2,1)S(1)}, bf16[1,24,6,192]{3,2,1,0:T(8,128)(2,1)S(1)}, u32[]{:S(2)}, u32[]{:S(2)}) collective-permute-start(bf16[1,24,6,192]{3,2,1,0:T(8,128)(2,1)S(1)} %fusion.154), channel_id=1, source_target_pairs={{0,1},{1,0},{2,3},{3,2},{4,5},{5,4},{6,7},{7,6},{8,9},{9,8},{10,11... | collective-permute-start | bytes 165896 | tf_op jit(solution)/shard_map/ppermute | solution.py:18
  161.4 9.1 %collective-permute-start.18 = (bf16[1,24,12,192]{3,2,1,0:T(8,128)(2,1)S(1)}, bf16[1,24,12,192]{3,2,1,0:T(8,128)(2,1)S(1)}, u32[]{:S(2)}, u32[]{:S(2)}) collective-permute-start(bf16[1,24,12,192]{3,2,1,0:T(8,128)(2,1)S(1)} %add_convert_fusion.4), channel_id=1, source_target_pairs={{8,0},{16,8},{24,16},{9,1},{17,9},{25,17},{10,2},{18,10},{26,18},{... | collective-permute-start | bytes 331784 | tf_op jit(solution)/shard_map/ppermute | solution.py:24
  170.4 0.7 copy-start.12
  171.2 1.0 copy-start.38
  171.3 0.7 copy-start.15
  174.8 0.9 copy-start.13
  175.8 2.2 copy-start.10
  175.8 2.2 copy-start.11
  176.1 3.9 %collective-permute-start.19 = (bf16[1,3,12,192]{3,2,1,0:T(8,128)(2,1)S(1)}, bf16[1,3,12,192]{3,2,1,0:T(8,128)(2,1)S(1)}, u32[]{:S(2)}, u32[]{:S(2)}) collective-permute-start(bf16[1,3,12,192]{3,2,1,0:T(8,128)(2,1)S(1)} %slice.220), channel_id=1, source_target_pairs={{0,6},{2,0},{4,2},{6,4},{1,7},{3,1},{5,3},{7,5},{8,14},{10,8},{12,... | collective-permute-start | bytes 41480 | tf_op jit(solution)/shard_map/ppermute | solution.py:18
  180.1 3.5 %collective-permute-start.20 = (bf16[1,24,6,192]{3,2,1,0:T(8,128)(2,1)S(1)}, bf16[1,24,6,192]{3,2,1,0:T(8,128)(2,1)S(1)}, u32[]{:S(2)}, u32[]{:S(2)}) collective-permute-start(bf16[1,24,6,192]{3,2,1,0:T(8,128)(2,1)S(1)} %get-tuple-element.34), channel_id=1, source_target_pairs={{0,1},{1,0},{2,3},{3,2},{4,5},{5,4},{6,7},{7,6},{8,9},{9,8},{10,11... | collective-permute-start | bytes 165896 | tf_op jit(solution)/shard_map/ppermute | solution.py:18
  184.7 0.9 copy-start.23
  185.6 1.8 copy-start.28
  190.2 0.9 copy-start.9
  191.5 0.9 copy-start.7
  191.6 4.5 %collective-permute-start.21 = (bf16[1,3,12,192]{3,2,1,0:T(8,128)(2,1)S(1)}, bf16[1,3,12,192]{3,2,1,0:T(8,128)(2,1)S(1)}, u32[]{:S(2)}, u32[]{:S(2)}) collective-permute-start(bf16[1,3,12,192]{3,2,1,0:T(8,128)(2,1)S(1)} %slice.223), channel_id=1, source_target_pairs={{0,2},{2,4},{4,6},{6,0},{1,3},{3,5},{5,7},{7,1},{8,10},{10,12},{12... | collective-permute-start | bytes 41480 | tf_op jit(solution)/shard_map/ppermute | solution.py:18
  193.6 3.9 %copy-start.5 = (bf16[288,192]{0,1:T(8,128)(2,1)S(1)}, bf16[288,192]{0,1:T(8,128)(2,1)}, u32[]{:S(2)}) copy-start(bf16[288,192]{0,1:T(8,128)(2,1)} %copy-done.4) | copy-start | bytes 331780
  196.2 3.5 %collective-permute-start.22 = (bf16[1,24,6,192]{3,2,1,0:T(8,128)(2,1)S(1)}, bf16[1,24,6,192]{3,2,1,0:T(8,128)(2,1)S(1)}, u32[]{:S(2)}, u32[]{:S(2)}) collective-permute-start(bf16[1,24,6,192]{3,2,1,0:T(8,128)(2,1)S(1)} %fusion.152), channel_id=1, source_target_pairs={{0,1},{1,0},{2,3},{3,2},{4,5},{5,4},{6,7},{7,6},{8,9},{9,8},{10,11... | collective-permute-start | bytes 165896 | tf_op jit(solution)/shard_map/ppermute | solution.py:18
  331.5 1.9 copy-start.19
  331.5 2.6 copy-start.17
  334.1 1.3 copy-start.16
Sparse Core Ops, SparseCore 0:
  198.5 132.9 all-reduce.3
where the time goes:
time: 345 us; the launch traced here: 343 us
  waiting for transfers between devices  152 us (44%)
  matrix products  48.2 us (14%)
  starting transfers between devices  41.2 us (12%)
  blocking collectives  39.6 us (11%)
  local copies, waits for them, and re-layouts  27.9 us (8%)
  other arithmetic  19.3 us (6%)
  between operations  15.4 us (4%)
    psum x1, waiting for transfers between devices, local(): lax.psum((parts[0], parts[1], parts[2], parts[3], parts[4], parts[5], par...  89.1 us
    ppermute x20, waiting for transfers between devices, shifted(): return lax.ppermute(value, axis, pairs)  45 us
    psum x1, blocking collectives, local(): lax.psum((parts[0], parts[1], parts[2], parts[3], parts[4], parts[5], par...  39.6 us
    ppermute x20, starting transfers between devices, shifted(): return lax.ppermute(value, axis, pairs)  25 us
    ppermute x3, waiting for transfers between devices, shifted_2(): return lax.ppermute(block, axis, route)  17.3 us
    ppermute x3, starting transfers between devices, shifted_2(): return lax.ppermute(block, axis, route)  16.2 us
    unnamed x82, local copies, waits for them, and re-layouts  13.5 us
    dot_general x4, matrix products, attend_back(): jnp.einsum('abhqk,abqhd->abkhd', d_scores, query, preferred_element_type=...  10.2 us
  transfers between devices with their start and end apart: 24, of which 23 were waited for; matrix products, arithmetic and copies ran while one was open for 3% of the time, Pallas kernels for 0%

commit v1 on v0

v1 whole, which is shorter than its diff:
```python
import functools

import jax
import jax.numpy as jnp
from jax import lax
from jax.experimental import pallas as pl
from jax.experimental.pallas import tpu as pltpu
from jax.sharding import PartitionSpec as P

HEADS = 6
HEAD_DIM = 32
WIN_LAT = 6
WIN_LON = 12
WIDTH = 192
MLP = 768
EPS = 1e-05

HALF = (WIN_LAT // 2) * (WIN_LON // 2)
PAD = 24
MESH = pl.DeviceIdType.MESH
F32 = jnp.float32
BF16 = jnp.bfloat16


def dot_nn(a, b):
    return jnp.dot(a, b, preferred_element_type=F32)


def dot_nt(a, b):
    return lax.dot_general(a, b, (((1,), (1,)), ((), ())), preferred_element_type=F32)


def dot_tn(a, b):
    return lax.dot_general(a, b, (((0,), (0,)), ((), ())), preferred_element_type=F32)


def mean_last(v):
    return jnp.sum(v, axis=-1, keepdims=True) * (1.0 / v.shape[-1])


def norm_parts(v):
    offset = v - mean_last(v)
    scale = lax.rsqrt(mean_last(offset * offset) + EPS)
    return offset * scale, scale


def norm_back(d_out, gain, hat, scale):
    d_hat = d_out * gain
    return scale * (d_hat - mean_last(d_hat) - hat * mean_last(d_hat * hat))


def head_masks():
    lane = lax.broadcasted_iota(jnp.int32, (1, WIDTH), 1)
    return [(lane >= h * HEAD_DIM) & (lane < (h + 1) * HEAD_DIM) for h in range(HEADS)]


def spread_heads(block, masks):
    return jnp.concatenate([jnp.where(m, block, 0.0) for m in masks], axis=0).astype(BF16)


def join_heads(stacked, masks):
    rows = stacked.shape[0] // HEADS
    total = jnp.where(masks[0], stacked[:rows], 0.0)
    for h in range(1, HEADS):
        total = jnp.where(masks[h], stacked[h * rows : (h + 1) * rows], total)
    return total


def interleave(first, second, bands):
    span = 2 * PAD
    parts = []
    for b in range(bands):
        parts += [first[b * span : (b + 1) * span], second[b * span : (b + 1) * span]]
    return jnp.concatenate(parts, axis=0)


def separate(field, bands):
    span = 2 * PAD
    firsts = [field[2 * b * span : (2 * b + 1) * span] for b in range(bands)]
    seconds = [field[(2 * b + 1) * span : (2 * b + 2) * span] for b in range(bands)]
    return jnp.concatenate(firsts + seconds, axis=0)


def kernel(
    sizes,
    bands,
    chunk,
    factor,
    x_ref,
    loss_ref,
    land_ref,
    embed_ref,
    ga_ref,
    gm_ref,
    wqkv_ref,
    wout_ref,
    wup_ref,
    wdown_ref,
    d_state_ref,
    g_qkv_ref,
    g_out_ref,
    g_up_ref,
    g_down_ref,
    g_small_ref,
    halo_src,
    halo_edge,
    halo_diag,
    halo_side,
    qm_ref,
    k_ref,
    v_ref,
    pt_ref,
    emb_hat,
    hid_hat,
    cot_ref,
    cot_src,
    cot_in,
    gelu_ref,
    act_ref,
    nmlp_ref,
    rolled_ref,
    mixed_ref,
    dqkv_ref,
    grad_ref,
    grad_b,
    lon_in,
    lon_sum,
    lon_b,
    lat_in,
    lat_sum,
    lat_b,
    sec_in,
    gathered,
    halo_send,
    halo_recv,
    cot_send,
    cot_recv,
    rs_send,
    rs_recv,
    ag_send,
    ag_recv,
):
    n_sec, n_lat, n_lon = sizes
    sec = lax.axis_index("section")
    lat = lax.axis_index("lat")
    lon = lax.axis_index("lon")

    def there(d_sec, d_lat, d_lon):
        return (
            lax.rem(sec + d_sec + n_sec, n_sec),
            lax.rem(lat + d_lat + n_lat, n_lat),
            lax.rem(lon + d_lon + n_lon, n_lon),
        )

    peers = [(d, 0, 0) for d in range(1, n_sec)]
    peers += [(0, d, 0) for d in range(1, n_lat)]
    peers += [(0, 0, d) for d in range(1, n_lon)]
    peers += [(0, 1, 1), (0, -1, -1)]
    barrier = pltpu.get_barrier_semaphore()
    for peer in peers:
        pl.semaphore_signal(barrier, inc=1, device_id=there(*peer), device_id_type=MESH)
    pl.semaphore_wait(barrier, len(peers))

    half = 2 * bands * PAD

    def halo(number, sign, edge_row, diag_row, side_row):
        copies = []
        for kind, (src, dst, target) in enumerate(
            (
                (halo_src.at[number, pl.ds(edge_row, 32)], halo_edge.at[number], (0, sign, 0)),
                (halo_src.at[number, pl.ds(diag_row, 32)], halo_diag.at[number], (0, sign, sign)),
                (halo_src.at[number, pl.ds(side_row, half)], halo_side.at[number], (0, 0, sign)),
            )
        ):
            copy = pltpu.make_async_remote_copy(
                src_ref=src,
                dst_ref=dst,
                send_sem=halo_send.at[number, kind],
                recv_sem=halo_recv.at[number, kind],
                device_id=there(*target),
                device_id_type=MESH,
            )
            copy.start()
            copies.append(copy)
        return copies

    def start_ahead(number, field):
        halo_src[number] = field.astype(BF16)
        return halo(number, -1, half, 0, 0)

    def end_ahead(number, copies):
        for copy in copies:
            copy.wait_recv()
        own = halo_src[number, pl.ds(half, half)].astype(F32)
        edge = halo_edge[number].astype(F32)
        diag = halo_diag[number].astype(F32)
        side = halo_side[number].astype(F32)
        first = jnp.concatenate([own[PAD:], edge[:PAD]], axis=0)
        second = jnp.concatenate([side[PAD:], diag[:PAD]], axis=0)
        return interleave(first, second, bands).astype(BF16)

    def start_behind(number, field):
        halo_src[number] = separate(field, bands).astype(BF16)
        return halo(number, 1, half - 32, 2 * half - 32, half)

    def end_behind(number, copies):
        for copy in copies:
            copy.wait_recv()
        own = halo_src[number, pl.ds(0, half)].astype(F32)
        edge = halo_edge[number].astype(F32)
        diag = halo_diag[number].astype(F32)
        side = halo_side[number].astype(F32)
        return jnp.concatenate(
            [diag[32 - PAD :], side[: half - PAD], edge[32 - PAD :], own[: half - PAD]], axis=0
        )

    masks = head_masks()
    window = 4 * PAD
    root = HEAD_DIM ** (-0.5)
    land = land_ref[...]
    gain_attn = ga_ref[...]
    gain_mlp = gm_ref[...]

    embedded = x_ref[...].astype(F32) + land * embed_ref[...]
    hat, emb_scale = norm_parts(embedded)
    emb_hat[...] = hat
    ahead_fwd = start_ahead(0, hat * gain_attn)

    key_id = lax.broadcasted_iota(jnp.int32, (window, HEADS * window), 0)
    query_id = lax.broadcasted_iota(jnp.int32, (window, HEADS * window), 1)
    for h in range(1, HEADS):
        query_id = jnp.where(
            lax.broadcasted_iota(jnp.int32, (window, HEADS * window), 1) >= h * window,
            lax.broadcasted_iota(jnp.int32, (window, HEADS * window), 1) - h * window,
            query_id,
        )

    def block_of(ids):
        return [ids >= n * PAD for n in range(1, 4)]

    k1, k2, k3 = block_of(key_id)
    q1, q2, q3 = block_of(query_id)
    key_start = jnp.where(k3, 3 * PAD, jnp.where(k2, 2 * PAD, jnp.where(k1, PAD, 0)))
    valid = jnp.where(key_id - key_start < HALF, 1.0, 0.0)
    key_late = jnp.where(k3, 1.0, jnp.where(k2, 0.0, jnp.where(k1, 1.0, 0.0)))
    query_late = jnp.where(q3, 1.0, jnp.where(q2, 0.0, jnp.where(q1, 1.0, 0.0)))
    differ = (key_late - query_late) * (key_late - query_late)
    wraps = jnp.where(lat == n_lat - 1, 1.0, 0.0)
    valid_edge = valid * (1.0 - differ * wraps)

    rolled = end_ahead(0, ahead_fwd)
    rolled_ref[...] = rolled
    w_q = wqkv_ref[:, 0:WIDTH]
    w_k = wqkv_ref[:, WIDTH : 2 * WIDTH]
    w_v = wqkv_ref[:, 2 * WIDTH : 3 * WIDTH]
    query = dot_nn(rolled, w_q)
    keys = dot_nn(rolled, w_k).astype(BF16)
    values = dot_nn(rolled, w_v).astype(BF16)
    k_ref[...] = keys
    v_ref[...] = values
    mixes = []
    for b in range(bands):
        rows = slice(b * window, (b + 1) * window)
        q_heads = spread_heads(query[rows], masks)
        qm_ref[b] = q_heads
        scores = dot_nt(keys[rows], q_heads) * root
        weights = jnp.exp(scores) * (valid_edge if b == bands - 1 else valid)
        probs = weights / jnp.sum(weights, axis=0, keepdims=True)
        pt_ref[b] = probs
        mixes.append(join_heads(dot_tn(probs.astype(BF16), values[rows]), masks))
    mixed = jnp.concatenate(mixes, axis=0).astype(BF16)
    mixed_ref[...] = mixed
    behind_fwd = start_behind(1, dot_nn(mixed, wout_ref[...]))

    hidden = embedded + end_behind(1, behind_fwd)
    hat2, hid_scale = norm_parts(hidden)
    hid_hat[...] = hat2
    normed_mlp = (hat2 * gain_mlp).astype(BF16)
    nmlp_ref[...] = normed_mlp
    pre = dot_nn(normed_mlp, wup_ref[...])
    cdf = 0.5 + 0.5 * lax.erf(pre * (0.5**0.5))
    act_ref[...] = (pre * cdf).astype(BF16)
    gelu_ref[...] = cdf + pre * (jnp.exp(pre * pre * -0.5) * 0.3989422804014327)

    cot_ref[...] = loss_ref[...].astype(F32)
    cot_copy = pltpu.make_async_remote_copy(
        src_ref=cot_src,
        dst_ref=cot_in,
        send_sem=cot_send,
        recv_sem=cot_recv,
        device_id=there(-1, 0, 0),
        device_id_type=MESH,
    )

    @pl.when(sec < n_sec - 1)
    def _():
        cot_copy.wait_recv()
        cot_ref[...] += cot_in[...].astype(F32)

    cot = cot_ref[...]
    cot_round = cot.astype(BF16)
    d_pre = (gelu_ref[...] * dot_nt(cot_round, wdown_ref[...])).astype(BF16)
    d_nmlp = dot_nt(d_pre, wup_ref[...])
    d_hidden = cot + norm_back(d_nmlp, gain_mlp, hid_hat[...], hid_scale)
    ahead_bwd = start_ahead(2, d_hidden)

    def put_tiles(first, block):
        height = block.shape[0]
        for t in range(block.shape[1] // 128):
            start = (first + t) * height
            grad_ref[start : start + height, :] = block[:, t * 128 : (t + 1) * 128]

    def put_small(index, vector):
        row = 18 * WIDTH + 2 * index
        grad_ref[row : row + 1, :] = vector[:, :128]
        grad_ref[row + 1 : row + 2, 0:64] = vector[:, 128:WIDTH]

    small_rows = grad_ref.shape[0] - 18 * WIDTH
    grad_ref[18 * WIDTH :, :] = jnp.zeros((small_rows, 128), F32)
    put_tiles(6, dot_tn(nmlp_ref[...], d_pre))
    put_tiles(12, dot_tn(cot_round, act_ref[...]))
    put_small(2, jnp.sum(d_nmlp * hid_hat[...], axis=0, keepdims=True))

    d_projected = end_ahead(2, ahead_bwd)
    d_mixed = dot_nt(d_projected, wout_ref[...])
    d_queries, d_keys, d_values = [], [], []
    for b in range(bands):
        rows = slice(b * window, (b + 1) * window)
        d_heads = spread_heads(d_mixed[rows], masks)
        probs = pt_ref[b]
        d_probs = dot_nt(v_ref[rows, :], d_heads)
        weighted = probs * d_probs
        d_scores = (
            (weighted - probs * jnp.sum(weighted, axis=0, keepdims=True)) * root
        ).astype(BF16)
        d_values.append(dot_nn(probs.astype(BF16), d_heads))
        d_keys.append(dot_nn(d_scores, qm_ref[b]))
        d_queries.append(join_heads(dot_tn(d_scores, k_ref[rows, :]), masks))
    d_q = jnp.concatenate(d_queries, axis=0).astype(BF16)
    d_k = jnp.concatenate(d_keys, axis=0).astype(BF16)
    d_v = jnp.concatenate(d_values, axis=0).astype(BF16)
    d_rolled = dot_nt(d_q, w_q) + dot_nt(d_k, w_k) + dot_nt(d_v, w_v)
    behind_bwd = start_behind(3, d_rolled)

    rolled = rolled_ref[...]
    put_tiles(0, jnp.concatenate([dot_tn(rolled, d_q), dot_tn(rolled, d_k)], axis=1))
    put_tiles(
        3,
        jnp.concatenate([dot_tn(rolled, d_v), dot_tn(mixed_ref[...], d_projected)], axis=1),
    )

    d_normed = end_behind(3, behind_bwd)
    hat = emb_hat[...]
    d_state = d_hidden + norm_back(d_normed, gain_attn, hat, emb_scale)
    cot_src[...] = d_state.astype(BF16)

    @pl.when(sec > 0)
    def _():
        cot_copy.start()

    d_state_ref[...] = d_state
    put_small(0, jnp.sum(d_state * land, axis=0, keepdims=True))
    put_small(1, jnp.sum(d_normed * hat, axis=0, keepdims=True))

    waits = list(ahead_fwd + behind_fwd + ahead_bwd + behind_bwd)
    sem = 0

    def reduce_stage(first_sem, axis, count, me, src, dst, rows):
        copies = []
        for d in range(1, count):
            step = [0, 0, 0]
            step[axis] = d
            target = there(*step)
            start = pl.multiple_of(target[axis] * rows, 16)
            copy = pltpu.make_async_remote_copy(
                src_ref=src.at[pl.ds(start, rows)],
                dst_ref=dst.at[d - 1],
                send_sem=rs_send.at[first_sem + d - 1],
                recv_sem=rs_recv.at[first_sem + d - 1],
                device_id=target,
                device_id_type=MESH,
            )
            copy.start()
            copies.append(copy)
        return copies

    def own_share(src, me, rows, dst, copies):
        total = src[pl.ds(pl.multiple_of(me * rows, 16), rows), :]
        for d, copy in enumerate(copies):
            copy.wait_recv()
            total = total + dst[d].astype(F32)
        return total

    lat_rows = chunk * n_sec
    lon_rows = lat_rows * n_lat
    grad_b[...] = grad_ref[...].astype(BF16)
    copies = reduce_stage(sem, 2, n_lon, lon, grad_b, lon_in, lon_rows)
    sem += n_lon - 1
    waits += copies
    lon_sum[...] = own_share(grad_ref, lon, lon_rows, lon_in, copies)
    lon_b[...] = lon_sum[...].astype(BF16)
    copies = reduce_stage(sem, 1, n_lat, lat, lon_b, lat_in, lat_rows)
    sem += n_lat - 1
    waits += copies
    lat_sum[...] = own_share(lon_sum, lat, lat_rows, lat_in, copies)
    lat_b[...] = lat_sum[...].astype(BF16)
    copies = reduce_stage(sem, 0, n_sec, sec, lat_b, sec_in, chunk)
    waits += copies
    final = own_share(lat_sum, sec, chunk, sec_in, copies)
    gathered[lon, lat, sec] = final.astype(BF16)

    def gather_stage(first_sem, axis, count, view):
        copies = []
        for d in range(1, count):
            step = [0, 0, 0]
            step[axis] = d
            copy = pltpu.make_async_remote_copy(
                src_ref=view,
                dst_ref=view,
                send_sem=ag_send.at[first_sem + d - 1],
                recv_sem=ag_recv.at[first_sem + d - 1],
                device_id=there(*step),
                device_id_type=MESH,
            )
            copy.start()
            copies.append(copy)
        for copy in copies:
            copy.wait_recv()
        return copies

    waits += gather_stage(0, 1, n_lat, gathered.at[lon, lat, sec])
    waits += gather_stage(n_lat - 1, 2, n_lon, gathered.at[lon, :, sec])
    waits += gather_stage(n_lat + n_lon - 2, 0, n_sec, gathered.at[:, :, sec])

    whole = gathered[...].reshape(n_lon * n_lat * n_sec * chunk, 128).astype(F32) * factor

    def tile(t):
        return whole[t * WIDTH : (t + 1) * WIDTH]

    for t in range(4):
        g_qkv_ref[:, t * 128 : (t + 1) * 128] = tile(t)
    g_qkv_ref[:, 512:576] = tile(4)[:, :64]
    g_out_ref[...] = jnp.concatenate([tile(4), tile(5)], axis=1)[:, 64:256]
    for t in range(6):
        g_up_ref[:, t * 128 : (t + 1) * 128] = tile(6 + t)
        g_down_ref[:, t * 128 : (t + 1) * 128] = tile(12 + t)
    g_small_ref[...] = whole[18 * WIDTH : 18 * WIDTH + 8]

    for copy in waits:
        copy.wait_send()

    @pl.when(sec > 0)
    def _():
        cot_copy.wait_send()


def to_blocks(field):
    height, breadth, width = field.shape
    grid = field.reshape(height // 3, 3, breadth // 6, 6, width).transpose(2, 0, 1, 3, 4)
    grid = grid.reshape(breadth // 6, height // 3, HALF, width)
    grid = jnp.pad(grid, ((0, 0), (0, 0), (0, PAD - HALF), (0, 0)))
    return grid.reshape(-1, width)


def from_blocks(rows, height, breadth):
    width = rows.shape[-1]
    grid = rows.reshape(breadth // 6, height // 3, PAD, width)[:, :, :HALF]
    grid = grid.reshape(breadth // 6, height // 3, 3, 6, width).transpose(1, 2, 0, 3, 4)
    return grid.reshape(height, breadth, width)


def local(
    sizes,
    states,
    loss_grads,
    land_sea,
    land_embed,
    gain_attn,
    gain_mlp,
    w_qkv,
    w_out,
    w_up,
    w_down,
):
    n_sec, n_lat, n_lon = sizes
    height, breadth = states.shape[2:4]
    bands = height // WIN_LAT
    tokens = (height // 3) * (breadth // 6) * PAD
    half = tokens // 2
    window = 4 * PAD
    devices = n_sec * n_lat * n_lon
    used = 18 * WIDTH + 8
    chunk = 16 * (-(-used // (16 * devices)))
    total = chunk * devices
    factor = float(n_sec * height * n_lat * breadth * n_lon) ** (-0.5)
    vmem = pltpu.VMEM
    sds = jax.ShapeDtypeStruct
    wide = HEADS * window
    n_rs = (n_sec - 1) + (n_lat - 1) + (n_lon - 1)
    d_state, g_qkv, g_out, g_up, g_down, g_small = pl.pallas_call(
        functools.partial(kernel, sizes, bands, chunk, factor),
        out_shape=(
            sds((tokens, WIDTH), F32),
            sds((WIDTH, 3 * WIDTH), F32),
            sds((WIDTH, WIDTH), F32),
            sds((WIDTH, MLP), F32),
            sds((WIDTH, MLP), F32),
            sds((8, 128), F32),
        ),
        in_specs=[pl.BlockSpec(memory_space=vmem)] * 10,
        out_specs=[pl.BlockSpec(memory_space=vmem)] * 6,
        scratch_shapes=[
            vmem((4, tokens, WIDTH), BF16),
            vmem((4, 32, WIDTH), BF16),
            vmem((4, 32, WIDTH), BF16),
            vmem((4, half, WIDTH), BF16),
            vmem((bands, wide, WIDTH), BF16),
            vmem((tokens, WIDTH), BF16),
            vmem((tokens, WIDTH), BF16),
            vmem((bands, window, wide), F32),
            vmem((tokens, WIDTH), F32),
            vmem((tokens, WIDTH), F32),
            vmem((tokens, WIDTH), F32),
            vmem((tokens, WIDTH), BF16),
            vmem((tokens, WIDTH), BF16),
            vmem((tokens, MLP), F32),
            vmem((tokens, MLP), BF16),
            vmem((tokens, WIDTH), BF16),
            vmem((tokens, WIDTH), BF16),
            vmem((tokens, WIDTH), BF16),
            vmem((tokens, WIDTH), BF16),
            vmem((total, 128), F32),
            vmem((total, 128), BF16),
            vmem((n_lon - 1, total // n_lon, 128), BF16),
            vmem((total // n_lon, 128), F32),
            vmem((total // n_lon, 128), BF16),
            vmem((n_lat - 1, chunk * n_sec, 128), BF16),
            vmem((chunk * n_sec, 128), F32),
            vmem((chunk * n_sec, 128), BF16),
            vmem((n_sec - 1, chunk, 128), BF16),
            vmem((n_lon, n_lat, n_sec, chunk, 128), BF16),
            pltpu.SemaphoreType.DMA((4, 3)),
            pltpu.SemaphoreType.DMA((4, 3)),
            pltpu.SemaphoreType.DMA,
            pltpu.SemaphoreType.DMA,
            pltpu.SemaphoreType.DMA((n_rs,)),
            pltpu.SemaphoreType.DMA((n_rs,)),
            pltpu.SemaphoreType.DMA((n_rs,)),
            pltpu.SemaphoreType.DMA((n_rs,)),
        ],
        compiler_params=pltpu.CompilerParams(
            collective_id=0, has_side_effects=True, vmem_limit_bytes=48 * 1024 * 1024
        ),
    )(
        to_blocks(states[0, 0]),
        to_blocks(loss_grads[0, 0]),
        to_blocks(land_sea.astype(F32)[:, :, None]),
        land_embed[None],
        gain_attn[None],
        gain_mlp[None],
        w_qkv,
        w_out,
        w_up,
        w_down,
    )
    small = g_small[:6].reshape(3, 256)[:, :WIDTH]
    return (
        from_blocks(d_state, height, breadth)[None, None],
        g_qkv,
        g_out,
        g_up,
        g_down.T,
        small[0],
        small[1],
        small[2],
    )


def solution(mesh):
    sizes = tuple(mesh.shape[name] for name in ("section", "lat", "lon"))
    cells = P("section", None, "lat", "lon", None)
    return jax.shard_map(
        functools.partial(local, sizes),
        mesh=mesh,
        in_specs=(cells, cells, P("lat", "lon")) + (P(),) * 7,
        out_specs=(cells,) + (P(),) * 7,
        check_vma=False,
    )
```

time: 345 us -> 112 us (0.32)
  waiting for transfers between devices: 152 us -> 0 us
  Pallas kernels: 0 us -> 101 us
  matrix products: 48.2 us -> 0 us
  starting transfers between devices: 41.2 us -> 0 us
  blocking collectives: 39.6 us -> 0 us
  local copies, waits for them, and re-layouts: 27.9 us -> 9.06 us
  other arithmetic: 19.3 us -> 0.7 us
  between operations: 15.4 us -> 0.77 us
    pallas_call x0 -> x1, Pallas kernels: none -> 101 us  [local(): pl.pallas_call(functools.partial(kernel, sizes, bands, chunk, factor), ou...]
    psum x1 -> x0, waiting for transfers between devices: 89.1 us -> none  [local(): lax.psum((parts[0], parts[1], parts[2], parts[3], parts[4], parts[5], par...]
    ppermute x23 -> x0, waiting for transfers between devices: 62.3 us -> none  [the longest x20 45 us: shifted(): return lax.ppermute(value, axis, pairs)]
    dot_general x37 -> x0, matrix products: 46.8 us -> none  [the longest x4 10.2 us: attend_back(): jnp.einsum('abhqk,abqhd->abkhd', d_scores, query, preferred_element_type=...]
    ppermute x23 -> x0, starting transfers between devices: 41.2 us -> none  [the longest x20 25 us: shifted(): return lax.ppermute(value, axis, pairs)]
    psum x1 -> x0, blocking collectives: 39.6 us -> none  [local(): lax.psum((parts[0], parts[1], parts[2], parts[3], parts[4], parts[5], par...]
    reduce_sum x21 -> x0, other arithmetic: 7.08 us -> none  [the longest x10 2.96 us: normalize(): return offset * lax.rsqrt(spread + EPS) * gain]
    unnamed x82 -> x27, local copies, waits for them, and re-layouts: 13.5 us -> 6.7 us
  transfers between devices with their start and end apart: 24 -> 0, of which waited for: 23 -> 0; matrix products, arithmetic and copies ran while one was open for 3% -> 0% of each run, Pallas kernels for 0% -> 0%
where the time goes in v1:
time: 112 us; the launch traced here: 111 us
  Pallas kernels  101 us (90%)
  local copies, waits for them, and re-layouts  9.06 us (8%)
    pallas_call x1, Pallas kernels, local(): pl.pallas_call(functools.partial(kernel, sizes, bands, chunk, factor), ou...  101 us
    unnamed x27, local copies, waits for them, and re-layouts  6.7 us

profile of v1, /device:TPU:1, one launch (start us, length us, event | category | flops | bytes accessed | tf_op | source)
XLA Modules:
  0.0 111.5 jit_solution(7694622399557108420)
XLA Ops:
  0.6 0.7 convert_element_type.8
  1.3 0.1 copy.27
  1.4 0.1 reshape_broadcast_in_dim.3
  1.5 0.0 copy-start.7
  1.5 0.1 copy.28
  1.6 0.1 copy.37
  1.7 0.1 reshape.52.land_ref
  1.9 0.6 copy-done.7
  2.4 0.1 reshape_squeeze.6
  2.6 0.0 copy-start.8
  2.6 0.9 copy-done.8
  3.5 0.1 reshape_squeeze.7
  3.6 0.0 copy-start.6
  3.7 0.9 copy-done.6
  4.6 0.0 copy-start
  4.6 0.0 copy-start.1
  4.6 0.0 copy-start.2
  4.6 0.0 copy-start.3
  4.6 0.0 copy-start.4
  4.6 0.0 copy-start.5
  4.6 0.2 copy.31.wdown_ref
  4.8 0.8 copy-done
  5.5 0.1 copy-done.1
  5.6 0.1 copy-done.2
  5.7 0.0 copy-done.3
  5.7 0.0 copy-done.4
  5.7 0.0 copy-done.5
  5.7 100.9 %shard_map.161 = (f32[384,192]{1,0:T(8,128)S(1)}, f32[192,576]{1,0:T(8,128)S(1)}, f32[192,192]{1,0:T(8,128)S(1)}, f32[192,768]{1,0:T(8,128)S(1)}, f32[192,768]{1,0:T(8,128)S(1)}, /*index=5*/f32[8,128]{1,0:T(8,128)S(1)}) custom-call(bf16[384,192]{1,0:T(8,128)(2,1)S(1)} %bitcast.35, bf16[384,192]{1,0:T(8,128)(2,1)S(1)} %bitcast.36, ...), custom_call_target="tpu_custom_call" | custom-call | tf_op jit(solution)/shard_map/pallas_call | solution.py:500
  106.6 0.1 copy.34
  106.7 0.6 fusion
  107.3 0.2 copy.33
  107.5 0.9 broadcast_in_dim_reshape.3
  108.4 0.8 copy.42
  109.2 0.7 copy.43
  109.8 0.8 copy.44
  110.7 0.8 copy.45
  (8 shorter events, 0.2 us)
Async XLA Ops:
  1.5 0.9 copy-start.7
  2.6 0.9 copy-start.8
  3.6 1.0 copy-start.6
  4.6 1.0 copy-start
  4.6 1.0 copy-start.1
  4.6 1.1 copy-start.2
  4.6 1.1 copy-start.3
  4.6 1.1 copy-start.4
  4.6 1.1 copy-start.5

commit v2 on v1

--- a/solution.py
+++ b/solution.py
@@ -84,10 +84,8 @@
 def kernel(
     sizes,
     bands,
-    chunk,
-    factor,
-    x_ref,
-    loss_ref,
+    plan,
+    field_ref,
     land_ref,
     embed_ref,
     ga_ref,
@@ -121,16 +119,27 @@
     rolled_ref,
     mixed_ref,
     dqkv_ref,
+    dproj_ref,
+    dpre_ref,
+    cotb_ref,
     grad_ref,
     grad_b,
-    lon_in,
-    lon_sum,
-    lon_b,
-    lat_in,
-    lat_sum,
-    lat_b,
-    sec_in,
-    gathered,
+    lon_in_a,
+    lon_sum_a,
+    lon_b_a,
+    lat_in_a,
+    lat_sum_a,
+    lat_b_a,
+    sec_in_a,
+    gathered_a,
+    lon_in_b,
+    lon_sum_b,
+    lon_b_b,
+    lat_in_b,
+    lat_sum_b,
+    lat_b_b,
+    sec_in_b,
+    gathered_b,
     halo_send,
     halo_recv,
     cot_send,
@@ -221,7 +230,7 @@
     gain_attn = ga_ref[...]
     gain_mlp = gm_ref[...]
 
-    embedded = x_ref[...].astype(F32) + land * embed_ref[...]
+    embedded = field_ref[0].astype(F32) + land * embed_ref[...]
     hat, emb_scale = norm_parts(embedded)
     emb_hat[...] = hat
     ahead_fwd = start_ahead(0, hat * gain_attn)
@@ -282,7 +291,7 @@
     act_ref[...] = (pre * cdf).astype(BF16)
     gelu_ref[...] = cdf + pre * (jnp.exp(pre * pre * -0.5) * 0.3989422804014327)
 
-    cot_ref[...] = loss_ref[...].astype(F32)
+    cot_ref[...] = field_ref[1].astype(F32)
     cot_copy = pltpu.make_async_remote_copy(
         src_ref=cot_src,
         dst_ref=cot_in,
@@ -304,21 +313,146 @@
     d_hidden = cot + norm_back(d_nmlp, gain_mlp, hid_hat[...], hid_scale)
     ahead_bwd = start_ahead(2, d_hidden)
 
+    base_b, split, chunks = plan
+    row_bases = (0, base_b)
+    bufs = (
+        (lon_in_a, lon_sum_a, lon_b_a, lat_in_a, lat_sum_a, lat_b_a, sec_in_a, gathered_a),
+        (lon_in_b, lon_sum_b, lon_b_b, lat_in_b, lat_sum_b, lat_b_b, sec_in_b, gathered_b),
+    )
+    axes = ((2, n_lon, lon), (1, n_lat, lat), (0, n_sec, sec))
+
+    def put_rows(start, block):
+        end = start + block.shape[0]
+        if start < split:
+            stop = min(end, split)
+            grad_ref[start:stop, :] = block[: stop - start]
+        if end > split:
+            begin = max(start, split)
+            place = base_b + begin - split
+            grad_ref[place : place + end - begin, :] = block[begin - start :]
+
     def put_tiles(first, block):
-        height = block.shape[0]
         for t in range(block.shape[1] // 128):
-            start = (first + t) * height
-            grad_ref[start : start + height, :] = block[:, t * 128 : (t + 1) * 128]
+            put_rows((first + t) * WIDTH, block[:, t * 128 : (t + 1) * 128])
 
     def put_small(index, vector):
-        row = 18 * WIDTH + 2 * index
+        row = base_b + 18 * WIDTH - split + 2 * index
         grad_ref[row : row + 1, :] = vector[:, :128]
         grad_ref[row + 1 : row + 2, 0:64] = vector[:, 128:WIDTH]
 
-    small_rows = grad_ref.shape[0] - 18 * WIDTH
-    grad_ref[18 * WIDTH :, :] = jnp.zeros((small_rows, 128), F32)
-    put_tiles(6, dot_tn(nmlp_ref[...], d_pre))
-    put_tiles(12, dot_tn(cot_round, act_ref[...]))
+    def share_rows(part, stage):
+        rows = chunks[part]
+        for _, count, _ in axes[stage + 1 :]:
+            rows *= count
+        return rows
+
+    def reduce_copies(part, stage):
+        src = (grad_b, bufs[part][2], bufs[part][5])[stage]
+        dst = (bufs[part][0], bufs[part][3], bufs[part][6])[stage]
+        base = row_bases[part] if stage == 0 else 0
+        rows = share_rows(part, stage)
+        axis, count, _ = axes[stage]
+        first_sem = sum(n - 1 for _, n, _ in axes[:stage])
+        copies = []
+        for d in range(1, count):
+            step = [0, 0, 0]
+            step[axis] = d
+            target = there(*step)
+            start = pl.multiple_of(base + target[axis] * rows, 16)
+            copies.append(
+                pltpu.make_async_remote_copy(
+                    src_ref=src.at[pl.ds(start, rows)],
+                    dst_ref=dst.at[d - 1],
+                    send_sem=rs_send.at[part, first_sem + d - 1],
+                    recv_sem=rs_recv.at[part, first_sem + d - 1],
+                    device_id=target,
+                    device_id_type=MESH,
+                )
+            )
+        return copies
+
+    def start_lon(part):
+        rows = share_rows(part, 0) * n_lon
+        span = slice(row_bases[part], row_bases[part] + rows)
+        grad_b[span, :] = grad_ref[span, :].astype(BF16)
+        for copy in reduce_copies(part, 0):
+            copy.start()
+
+    def own_share(part, stage):
+        src = (grad_ref, bufs[part][1], bufs[part][4])[stage]
+        dst = (bufs[part][0], bufs[part][3], bufs[part][6])[stage]
+        base = row_bases[part] if stage == 0 else 0
+        rows = share_rows(part, stage)
+        total = src[pl.ds(pl.multiple_of(base + axes[stage][2] * rows, 16), rows), :]
+        for d, copy in enumerate(reduce_copies(part, stage)):
+            copy.wait_recv()
+            total = total + dst[d].astype(F32)
+        return total
+
+    def next_stage(part, stage):
+        total = own_share(part, stage)
+        if stage == 2:
+            bufs[part][7][lon, lat, sec] = total.astype(BF16)
+            return
+        bufs[part][1 + 3 * stage][...] = total
+        bufs[part][2 + 3 * stage][...] = total.astype(BF16)
+        for copy in reduce_copies(part, stage + 1):
+            copy.start()
+
+    def gather_copies(part, stage):
+        gathered = bufs[part][7]
+        own = (sec, lat, lon)
+        first_sem = (0, n_lat - 1, n_lat + n_lon - 2, n_lat + n_lon)[stage]
+        if stage == 0:
+            view = gathered.at[lon, lat, sec]
+            targets = [there(0, d, 0) for d in range(1, n_lat)]
+        elif stage == 1:
+            view = gathered.at[lon, :, sec]
+            targets = [there(0, 0, d) for d in range(1, n_lon)]
+        elif n_sec != 4:
+            view = gathered.at[:, :, sec]
+            targets = [there(d, 0, 0) for d in range(1, n_sec)] if stage == 2 else []
+        else:
+            sibling = (sec + 1 - 2 * lax.rem(sec, 2), own[1], own[2])
+            across = there(2, 0, 0)
+            view = gathered.at[:, :, sec if stage == 2 else across[0]]
+            targets = [across, sibling] if stage == 2 else [sibling]
+        return [
+            pltpu.make_async_remote_copy(
+                src_ref=view,
+                dst_ref=view,
+                send_sem=ag_send.at[part, first_sem + n],
+                recv_sem=ag_recv.at[part, first_sem + n],
+                device_id=target,
+                device_id_type=MESH,
+            )
+            for n, target in enumerate(targets)
+        ]
+
+    def start_gather(part, stage):
+        for copy in gather_copies(part, stage):
+            copy.start()
+
+    def end_gather(part, stage):
+        for copy in gather_copies(part, stage):
+            copy.wait_recv()
+
+    tail = base_b + 18 * WIDTH - split
+    grad_ref[tail:, :] = jnp.zeros((grad_ref.shape[0] - tail, 128), F32)
+    if split < base_b:
+        grad_ref[split:base_b, :] = jnp.zeros((base_b - split, 128), F32)
+    dpre_ref[...] = d_pre
+    cotb_ref[...] = cot_round
+
+    def mlp_grads():
+        put_tiles(0, dot_tn(nmlp_ref[...], dpre_ref[...]))
+        put_tiles(6, dot_tn(cotb_ref[...], act_ref[...]))
+        start_lon(0)
+
+    @pl.when(sec == 0)
+    def _():
+        mlp_grads()
+
     put_small(2, jnp.sum(d_nmlp * hid_hat[...], axis=0, keepdims=True))
 
     d_projected = end_ahead(2, ahead_bwd)
@@ -342,12 +476,22 @@
     d_rolled = dot_nt(d_q, w_q) + dot_nt(d_k, w_k) + dot_nt(d_v, w_v)
     behind_bwd = start_behind(3, d_rolled)
 
-    rolled = rolled_ref[...]
-    put_tiles(0, jnp.concatenate([dot_tn(rolled, d_q), dot_tn(rolled, d_k)], axis=1))
-    put_tiles(
-        3,
-        jnp.concatenate([dot_tn(rolled, d_v), dot_tn(mixed_ref[...], d_projected)], axis=1),
-    )
+    dproj_ref[...] = d_projected
+    dqkv_ref[0] = d_q
+    dqkv_ref[1] = d_k
+    dqkv_ref[2] = d_v
+
+    def attn_grads():
+        rolled = rolled_ref[...]
+        g_q, g_k, g_v = (dot_tn(rolled, dqkv_ref[n]) for n in range(3))
+        put_tiles(12, jnp.concatenate([g_q, g_k], axis=1))
+        g_o = dot_tn(mixed_ref[...], dproj_ref[...])
+        put_tiles(15, jnp.concatenate([g_v, g_o], axis=1))
+        next_stage(0, 0)
+
+    @pl.when(sec == 0)
+    def _():
+        attn_grads()
 
     d_normed = end_behind(3, behind_bwd)
     hat = emb_hat[...]
@@ -357,97 +501,66 @@
     @pl.when(sec > 0)
     def _():
         cot_copy.start()
+        mlp_grads()
+        attn_grads()
 
     d_state_ref[...] = d_state
     put_small(0, jnp.sum(d_state * land, axis=0, keepdims=True))
     put_small(1, jnp.sum(d_normed * hat, axis=0, keepdims=True))
 
-    waits = list(ahead_fwd + behind_fwd + ahead_bwd + behind_bwd)
-    sem = 0
-
-    def reduce_stage(first_sem, axis, count, me, src, dst, rows):
-        copies = []
-        for d in range(1, count):
-            step = [0, 0, 0]
-            step[axis] = d
-            target = there(*step)
-            start = pl.multiple_of(target[axis] * rows, 16)
-            copy = pltpu.make_async_remote_copy(
-                src_ref=src.at[pl.ds(start, rows)],
-                dst_ref=dst.at[d - 1],
-                send_sem=rs_send.at[first_sem + d - 1],
-                recv_sem=rs_recv.at[first_sem + d - 1],
-                device_id=target,
-                device_id_type=MESH,
-            )
-            copy.start()
-            copies.append(copy)
-        return copies
-
-    def own_share(src, me, rows, dst, copies):
-        total = src[pl.ds(pl.multiple_of(me * rows, 16), rows), :]
-        for d, copy in enumerate(copies):
-            copy.wait_recv()
-            total = total + dst[d].astype(F32)
-        return total
-
-    lat_rows = chunk * n_sec
-    lon_rows = lat_rows * n_lat
-    grad_b[...] = grad_ref[...].astype(BF16)
-    copies = reduce_stage(sem, 2, n_lon, lon, grad_b, lon_in, lon_rows)
-    sem += n_lon - 1
-    waits += copies
-    lon_sum[...] = own_share(grad_ref, lon, lon_rows, lon_in, copies)
-    lon_b[...] = lon_sum[...].astype(BF16)
-    copies = reduce_stage(sem, 1, n_lat, lat, lon_b, lat_in, lat_rows)
-    sem += n_lat - 1
-    waits += copies
-    lat_sum[...] = own_share(lon_sum, lat, lat_rows, lat_in, copies)
-    lat_b[...] = lat_sum[...].astype(BF16)
-    copies = reduce_stage(sem, 0, n_sec, sec, lat_b, sec_in, chunk)
-    waits += copies
-    final = own_share(lat_sum, sec, chunk, sec_in, copies)
-    gathered[lon, lat, sec] = final.astype(BF16)
-
-    def gather_stage(first_sem, axis, count, view):
-        copies = []
-        for d in range(1, count):
-            step = [0, 0, 0]
-            step[axis] = d
-            copy = pltpu.make_async_remote_copy(
-                src_ref=view,
-                dst_ref=view,
-                send_sem=ag_send.at[first_sem + d - 1],
-                recv_sem=ag_recv.at[first_sem + d - 1],
-                device_id=there(*step),
-                device_id_type=MESH,
-            )
-            copy.start()
-            copies.append(copy)
-        for copy in copies:
-            copy.wait_recv()
-        return copies
-
-    waits += gather_stage(0, 1, n_lat, gathered.at[lon, lat, sec])
-    waits += gather_stage(n_lat - 1, 2, n_lon, gathered.at[lon, :, sec])
-    waits += gather_stage(n_lat + n_lon - 2, 0, n_sec, gathered.at[:, :, sec])
-
-    whole = gathered[...].reshape(n_lon * n_lat * n_sec * chunk, 128).astype(F32) * factor
+    start_lon(1)
+    next_stage(0, 1)
+    next_stage(1, 0)
+    next_stage(0, 2)
+    start_gather(0, 0)
+    next_stage(1, 1)
+    end_gather(0, 0)
+    start_gather(0, 1)
+    next_stage(1, 2)
+    start_gather(1, 0)
+    end_gather(0, 1)
+    start_gather(0, 2)
+    end_gather(1, 0)
+    start_gather(1, 1)
+    end_gather(1, 1)
+    start_gather(1, 2)
+    end_gather(0, 2)
+    start_gather(0, 3)
+    end_gather(1, 2)
+    start_gather(1, 3)
+    end_gather(0, 3)
+    whole_a = gathered_a[...].reshape(-1, 128)[:split]
+    end_gather(1, 3)
+    whole_b = gathered_b[...].reshape(-1, 128)
 
     def tile(t):
-        return whole[t * WIDTH : (t + 1) * WIDTH]
-
+        start, end = t * WIDTH, (t + 1) * WIDTH
+        if end <= split:
+            return whole_a[start:end]
+        if start >= split:
+            return whole_b[start - split : end - split]
+        return jnp.concatenate([whole_a[start:], whole_b[: end - split]], axis=0)
+
+    for t in range(6):
+        g_up_ref[:, t * 128 : (t + 1) * 128] = tile(t)
+        g_down_ref[:, t * 128 : (t + 1) * 128] = tile(6 + t)
     for t in range(4):
-        g_qkv_ref[:, t * 128 : (t + 1) * 128] = tile(t)
-    g_qkv_ref[:, 512:576] = tile(4)[:, :64]
-    g_out_ref[...] = jnp.concatenate([tile(4), tile(5)], axis=1)[:, 64:256]
-    for t in range(6):
-        g_up_ref[:, t * 128 : (t + 1) * 128] = tile(6 + t)
-        g_down_ref[:, t * 128 : (t + 1) * 128] = tile(12 + t)
-    g_small_ref[...] = whole[18 * WIDTH : 18 * WIDTH + 8]
-
-    for copy in waits:
+        g_qkv_ref[:, t * 128 : (t + 1) * 128] = tile(12 + t)
+    g_qkv_ref[:, 512:576] = tile(16)[:, :64]
+    last = jnp.concatenate([tile(16), tile(17)], axis=1).astype(F32)
+    g_out_ref[...] = last[:, 64:256].astype(BF16)
+    small = 18 * WIDTH - split
+    g_small_ref[...] = whole_b[small : small + 16].astype(F32)
+
+    for copy in ahead_fwd + behind_fwd + ahead_bwd + behind_bwd:
         copy.wait_send()
+    for part in range(2):
+        for stage in range(3):
+            for copy in reduce_copies(part, stage):
+                copy.wait_send()
+        for stage in range(4):
+            for copy in gather_copies(part, stage):
+                copy.wait_send()
 
     @pl.when(sec > 0)
     def _():
@@ -455,11 +568,12 @@
 
 
 def to_blocks(field):
-    height, breadth, width = field.shape
-    grid = field.reshape(height // 3, 3, breadth // 6, 6, width).transpose(2, 0, 1, 3, 4)
-    grid = grid.reshape(breadth // 6, height // 3, HALF, width)
-    grid = jnp.pad(grid, ((0, 0), (0, 0), (0, PAD - HALF), (0, 0)))
-    return grid.reshape(-1, width)
+    count, height, breadth, width = field.shape
+    grid = field.reshape(count, height // 3, 3, breadth // 6, 6, width)
+    grid = grid.transpose(0, 3, 1, 2, 4, 5)
+    grid = grid.reshape(count, breadth // 6, height // 3, HALF, width)
+    grid = jnp.pad(grid, ((0, 0), (0, 0), (0, 0), (0, PAD - HALF), (0, 0)))
+    return grid.reshape(count, -1, width)
 
 
 def from_blocks(rows, height, breadth):
@@ -467,6 +581,22 @@
     grid = rows.reshape(breadth // 6, height // 3, PAD, width)[:, :, :HALF]
     grid = grid.reshape(breadth // 6, height // 3, 3, 6, width).transpose(1, 2, 0, 3, 4)
     return grid.reshape(height, breadth, width)
+
+
+def reduce_scratch(chunk, sizes):
+    n_sec, n_lat, n_lon = sizes
+    lat_rows = chunk * n_sec
+    lon_rows = lat_rows * n_lat
+    return [
+        pltpu.VMEM((n_lon - 1, lon_rows, 128), BF16),
+        pltpu.VMEM((lon_rows, 128), F32),
+        pltpu.VMEM((lon_rows, 128), BF16),
+        pltpu.VMEM((n_lat - 1, lat_rows, 128), BF16),
+        pltpu.VMEM((lat_rows, 128), F32),
+        pltpu.VMEM((lat_rows, 128), BF16),
+        pltpu.VMEM((n_sec - 1, chunk, 128), BF16),
+        pltpu.VMEM((n_lon, n_lat, n_sec, chunk, 128), BF16),
+    ]
 
 
 def local(
@@ -489,25 +619,30 @@
     half = tokens // 2
     window = 4 * PAD
     devices = n_sec * n_lat * n_lon
-    used = 18 * WIDTH + 8
-    chunk = 16 * (-(-used // (16 * devices)))
-    total = chunk * devices
+    unit = 16 * devices
+    mlp_rows = 12 * WIDTH
+    units_a = max(1, mlp_rows // unit)
+    split = min(mlp_rows, units_a * unit)
+    units_b = -(-(18 * WIDTH + 16 - split) // unit)
+    chunks = (16 * units_a, 16 * units_b)
+    plan = (units_a * unit, split, chunks)
+    total = (units_a + units_b) * unit
     factor = float(n_sec * height * n_lat * breadth * n_lon) ** (-0.5)
     vmem = pltpu.VMEM
     sds = jax.ShapeDtypeStruct
     wide = HEADS * window
     n_rs = (n_sec - 1) + (n_lat - 1) + (n_lon - 1)
     d_state, g_qkv, g_out, g_up, g_down, g_small = pl.pallas_call(
-        functools.partial(kernel, sizes, bands, chunk, factor),
+        functools.partial(kernel, sizes, bands, plan),
         out_shape=(
             sds((tokens, WIDTH), F32),
-            sds((WIDTH, 3 * WIDTH), F32),
-            sds((WIDTH, WIDTH), F32),
-            sds((WIDTH, MLP), F32),
-            sds((WIDTH, MLP), F32),
-            sds((8, 128), F32),
+            sds((WIDTH, 3 * WIDTH), BF16),
+            sds((WIDTH, WIDTH), BF16),
+            sds((WIDTH, MLP), BF16),
+            sds((WIDTH, MLP), BF16),
+            sds((16, 128), F32),
         ),
-        in_specs=[pl.BlockSpec(memory_space=vmem)] * 10,
+        in_specs=[pl.BlockSpec(memory_space=vmem)] * 9,
         out_specs=[pl.BlockSpec(memory_space=vmem)] * 6,
         scratch_shapes=[
             vmem((4, tokens, WIDTH), BF16),
@@ -528,33 +663,29 @@
             vmem((tokens, WIDTH), BF16),
             vmem((tokens, WIDTH), BF16),
             vmem((tokens, WIDTH), BF16),
+            vmem((3, tokens, WIDTH), BF16),
+            vmem((tokens, WIDTH), BF16),
+            vmem((tokens, MLP), BF16),
             vmem((tokens, WIDTH), BF16),
             vmem((total, 128), F32),
             vmem((total, 128), BF16),
-            vmem((n_lon - 1, total // n_lon, 128), BF16),
-            vmem((total // n_lon, 128), F32),
-            vmem((total // n_lon, 128), BF16),
-            vmem((n_lat - 1, chunk * n_sec, 128), BF16),
-            vmem((chunk * n_sec, 128), F32),
-            vmem((chunk * n_sec, 128), BF16),
-            vmem((n_sec - 1, chunk, 128), BF16),
-            vmem((n_lon, n_lat, n_sec, chunk, 128), BF16),
+            *reduce_scratch(chunks[0], sizes),
+            *reduce_scratch(chunks[1], sizes),
             pltpu.SemaphoreType.DMA((4, 3)),
             pltpu.SemaphoreType.DMA((4, 3)),
             pltpu.SemaphoreType.DMA,
             pltpu.SemaphoreType.DMA,
-            pltpu.SemaphoreType.DMA((n_rs,)),
-            pltpu.SemaphoreType.DMA((n_rs,)),
-            pltpu.SemaphoreType.DMA((n_rs,)),
-            pltpu.SemaphoreType.DMA((n_rs,)),
+            pltpu.SemaphoreType.DMA((2, n_rs)),
+            pltpu.SemaphoreType.DMA((2, n_rs)),
+            pltpu.SemaphoreType.DMA((2, n_rs)),
+            pltpu.SemaphoreType.DMA((2, n_rs)),
         ],
         compiler_params=pltpu.CompilerParams(
             collective_id=0, has_side_effects=True, vmem_limit_bytes=48 * 1024 * 1024
         ),
     )(
-        to_blocks(states[0, 0]),
-        to_blocks(loss_grads[0, 0]),
-        to_blocks(land_sea.astype(F32)[:, :, None]),
+        to_blocks(jnp.concatenate([states[0], loss_grads[0]])),
+        to_blocks(land_sea.astype(F32)[None, :, :, None])[0],
         land_embed[None],
         gain_attn[None],
         gain_mlp[None],
@@ -563,13 +694,13 @@
         w_up,
         w_down,
     )
-    small = g_small[:6].reshape(3, 256)[:, :WIDTH]
+    small = g_small[:6].reshape(3, 256)[:, :WIDTH] * factor
     return (
         from_blocks(d_state, height, breadth)[None, None],
-        g_qkv,
-        g_out,
-        g_up,
-        g_down.T,
+        g_qkv.astype(F32) * factor,
+        g_out.astype(F32) * factor,
+        g_up.astype(F32) * factor,
+        g_down.T.astype(F32) * factor,
         small[0],
         small[1],
         small[2],

time: 112 us -> 98.7 us (0.88)
  Pallas kernels: 101 us -> 89 us
  local copies, waits for them, and re-layouts: 9.06 us -> 5.8 us
  other arithmetic: 0.7 us -> 2.93 us
    pallas_call x1, Pallas kernels: 101 us -> 89 us  [local(): pl.pallas_call(functools.partial(kernel, sizes, bands, plan), out_shape=(...]
    unnamed x27 -> x22, local copies, waits for them, and re-layouts: 6.7 us -> 2.5 us
    mul x0 -> x4, other arithmetic: none -> 2.62 us  [the longest x1 1.1 us: local(): g_down.T.astype(F32) * factor]
where the time goes in v2:
time: 98.7 us; the launch traced here: 98.5 us
  Pallas kernels  89 us (90%)
  local copies, waits for them, and re-layouts  5.8 us (6%)
  other arithmetic  2.93 us (3%)
    pallas_call x1, Pallas kernels, local(): pl.pallas_call(functools.partial(kernel, sizes, bands, plan), out_shape=(...  89 us
    unnamed x22, local copies, waits for them, and re-layouts  2.5 us

profile of v2, /device:TPU:1, one launch (start us, length us, event | category | flops | bytes accessed | tf_op | source)
XLA Modules:
  0.0 98.5 jit_solution(5507852300674233989)
XLA Ops:
  0.6 0.0 copy-start.7
  0.6 1.0 %concatenate.8 = bf16[1,8,3,2,6,192]{5,2,1,4,3,0:T(4,128)(2,1)S(1)} reshape(bf16[1,1,24,12,192]{4,2,3,1,0:T(8,128)(2,1)} %param.10) | data formatting | bytes 221184 | tf_op jit(solution)/shard_map/concatenate | solution.py:687
  1.7 0.0 copy-done.7
  1.7 0.1 concatenate.9
  1.8 0.3 maximum_bitcast_fusion
  2.1 0.1 copy.32
  2.2 0.0 copy-start.6
  2.2 0.1 pad.8.clone
  2.3 0.9 copy-done.6
  3.2 0.0 copy-start.8
  3.2 0.0 copy-start.1
  3.2 0.0 copy-start.2
  3.2 0.2 copy.28.wdown_ref
  3.4 0.5 copy-done.8
  3.9 0.0 copy-start
  3.9 0.1 copy.24
  4.0 0.1 reshape_broadcast_in_dim.3
  4.1 0.1 copy.25
  4.2 0.1 copy.33
  4.3 0.0 copy-start.4
  4.3 0.0 copy-start.5
  4.3 0.1 squeeze_reshape.4.land_ref
  4.4 0.0 copy-start.3
  4.4 0.0 copy-done.1
  4.4 0.0 copy-done.2
  4.4 0.5 copy-done
  4.9 0.1 copy-done.4
  5.0 0.0 copy-done.5
  5.0 0.1 copy-done.3
  5.1 89.0 %shard_map.161 = (f32[384,192]{1,0:T(8,128)S(1)}, bf16[192,576]{1,0:T(8,128)(2,1)S(1)}, bf16[192,192]{1,0:T(8,128)(2,1)S(1)}, bf16[192,768]{1,0:T(8,128)(2,1)S(1...) custom-call(bf16[2,384,192]{2,1,0:T(8,128)(2,1)S(1)} %bitcast.33, f32[384,1]{1,0:T(8,128)S(1)} %squeeze_reshape.4.land_ref, ...), custom_call_target="tpu_custom_call" | custom-call | tf_op jit(solution)/shard_map/pallas_call | solution.py:635
  94.1 1.1 %multiply_bitcast_fusion = (f32[768,192]{0,1:T(8,128)}, f32[192,768]{1,0:T(8,128)}) fusion(bf16[192,768]{1,0:T(8,128)(2,1)S(1)} %get-tuple-element.18, bf16[192,768]{1,0:T(8,128)(2,1)S(1)} %get-tuple-element.17), kind=kLoop, calls=%fused_computation | loop fusion | flops 589824 | bytes 1769472 | tf_op jit(solution)/shard_map/mul | solution.py:703
  95.2 0.6 fusion
  95.8 0.1 copy.31
  95.9 0.2 copy.30
  96.1 0.9 broadcast_in_dim_reshape.3
  97.0 0.8 convert_multiply_fusion.1
  97.8 0.7 convert_multiply_fusion.2
  (6 shorter events, 0.1 us)
Async XLA Ops:
  0.6 1.0 %copy-start.7 = (bf16[1,1,24,12,192]{4,2,3,1,0:T(8,128)(2,1)S(1)}, bf16[1,1,24,12,192]{4,2,3,1,0:T(8,128)(2,1)}, u32[]{:S(2)}) copy-start(bf16[1,1,24,12,192]{4,2,3,1,0:T(8,128)(2,1)} %param.11) | copy-start | bytes 331780
  2.2 1.0 copy-start.6
  3.2 0.7 copy-start.8
  3.2 1.2 %copy-start.1 = (bf16[192,576]{1,0:T(8,128)(2,1)S(1)}, bf16[192,576]{1,0:T(8,128)(2,1)}, u32[]{:S(2)}) copy-start(bf16[192,576]{1,0:T(8,128)(2,1)} %wqkv_ref.1) | copy-start | bytes 663556
  3.2 1.2 %copy-start.2 = (bf16[192,192]{1,0:T(8,128)(2,1)S(1)}, bf16[192,192]{1,0:T(8,128)(2,1)}, u32[]{:S(2)}) copy-start(bf16[192,192]{1,0:T(8,128)(2,1)} %wout_ref.1) | copy-start | bytes 221188
  3.9 1.0 %copy-start = (bf16[192,768]{1,0:T(8,128)(2,1)S(1)}, bf16[192,768]{1,0:T(8,128)(2,1)}, u32[]{:S(2)}) copy-start(bf16[192,768]{1,0:T(8,128)(2,1)} %wup_ref.1) | copy-start | bytes 884740
  4.3 0.7 copy-start.4
  4.3 0.7 copy-start.5
  4.4 0.7 copy-start.3
